TPU v7x, 32 devices: a whole 2x2x4 slice. The times are simulated.
32 devices in a mesh: groups: 2 (over x), row: 8 (over z, y), col: 2 (over core).
Axes of the slice: x: 2, y: 2, z: 4, core: 2. Of those that a mesh axis runs over, the one named last changes fastest.
Arguments:
- queries: bfloat16 [4096, 2560], P(('groups', 'row', 'col')), parts along dimension 0, may hold values from -32 to 32
- keys: bfloat16 [4096, 2560], P(('groups', 'row', 'col')), parts along dimension 0, may hold values from -6 to 6
- values: bfloat16 [4096, 2560], P(('groups', 'row', 'col')), parts along dimension 0, may hold values from -6 to 6
- pattern: int32 [16, 5], P('groups'), parts along dimension 0, may hold values from 0 to 1, as said below
Outputs:
- attended: bfloat16 [4096, 2560], P(('groups', 'row', 'col')), parts along dimension 0
There are 2 independent parts, one for each index of `groups`. A program takes and returns all parts, laid end to end along the dimension named above; each array names one. Nothing has to cross between parts.
Inputs may be any that keep to these rules, and one draw needn't show every extreme that they name: pattern[r, 0] is 1; pattern[r, j] is 0 where r + off_j lies outside 0 .. 7, or where off_j is -1 or +1 and r + off_j lies in another band of 4 tile rows.
All inputs are finite; a program needn't handle non-finite values.
Results may differ from a plain program's by a relative error of at most 0.0045.
Values may be sent and summed in bfloat16 or wider, within the bound.
A program may use at most 64 MiB of HBM per device.

v0:
```python
import jax
import jax.numpy as jnp
from jax import lax
from jax.sharding import PartitionSpec as P

HEADS = 20
HD = 128
TILE_H = 4


far_below = -1e30


def passed_along(value, axis, by):
    count = lax.axis_size(axis)
    pairs = [(i, i + by) for i in range(count) if 0 <= i + by < count]
    return lax.ppermute(value, axis, pairs)


def block_terms(query_heads, key_block, value_block):
    key_heads = key_block.reshape(key_block.shape[0], HEADS, HD)
    value_heads = value_block.reshape(value_block.shape[0], HEADS, HD)
    scores = jnp.einsum(
        "qhd,khd->hqk", query_heads, key_heads, preferred_element_type=jnp.float32
    ) * HD ** (-0.5)
    block_max = jnp.max(scores, axis=2)
    weights = jnp.exp(scores - block_max[:, :, None])
    block_total = jnp.sum(weights, axis=2)
    block_out = jnp.einsum(
        "hqk,khd->qhd",
        weights.astype(jnp.bfloat16),
        value_heads,
        preferred_element_type=jnp.float32,
    )
    return (block_out, block_max.T, block_total.T)


def skipped(rows_here):
    return (
        jnp.zeros((rows_here, HEADS, HD), jnp.float32),
        jnp.full((rows_here, HEADS), far_below, jnp.float32),
        jnp.zeros((rows_here, HEADS), jnp.float32),
    )


def guarded(is_live, query_heads, key_block, value_block):
    rows_here = query_heads.shape[0]
    return lax.cond(
        is_live,
        lambda a, b, c: block_terms(a, b, c),
        lambda a, b, c: skipped(rows_here),
        query_heads,
        key_block,
        value_block,
    )


def keep_live(is_live, terms):
    rows_here = terms[0].shape[0]
    empty_terms = skipped(rows_here)
    return tuple(
        (jnp.where(is_live, given, fallback) for given, fallback in zip(terms, empty_terms))
    )


def combine(pieces):
    outs_all = jnp.stack([piece[0] for piece in pieces])
    maxes_all = jnp.stack([piece[1] for piece in pieces])
    totals_all = jnp.stack([piece[2] for piece in pieces])
    top_max = jnp.max(maxes_all, axis=0)
    factors = jnp.exp(maxes_all - top_max)
    numerator = jnp.sum(factors[..., None] * outs_all, axis=0)
    denominator = jnp.sum(factors * totals_all, axis=0)
    return numerator / denominator[..., None]


def shards(queries, keys, values, pattern):
    rows_here = queries.shape[0]
    width = queries.shape[1]
    row_index = lax.axis_index("row")
    row_count = lax.axis_size("row")
    query_heads = queries.reshape(rows_here, HEADS, HD)
    key_row, value_row = (
        lax.all_gather(keys, "col", axis=0, tiled=True),
        lax.all_gather(values, "col", axis=0, tiled=True),
    )
    offsets = [0, -1, 1, -TILE_H, TILE_H]
    pieces = []
    for number in range(5):
        offset = offsets[number]
        is_live = pattern[row_index, number] == 1
        if offset == 0:
            pieces.append(guarded(is_live, query_heads, key_row, value_row))
        else:
            visitors = passed_along(query_heads, "row", offset)
            source = row_index - offset
            inside = (source >= 0) & (source < row_count)
            source_live = inside & (pattern[jnp.clip(source, 0, row_count - 1), number] == 1)
            terms = guarded(source_live, visitors, key_row, value_row)
            returned = passed_along(terms, "row", -offset)
            pieces.append(keep_live(is_live, returned))
    attended = combine(pieces).astype(jnp.bfloat16)
    return attended.reshape(rows_here, width)


def solution(mesh):
    placed = (
        P(("groups", "row", "col"), None),
        P(("groups", "row", "col"), None),
        P(("groups", "row", "col"), None),
        P("groups", None),
    )
    return jax.shard_map(
        shards,
        mesh=mesh,
        in_specs=placed,
        out_specs=P(("groups", "row", "col"), None),
        check_vma=False,
    )
```

profile of v0, /device:TPU:0, one launch (start us, length us, event | category | flops | bytes accessed | tf_op | source)
XLA Modules:
  0.0 198.1 jit_solution(4693203722182766323)
XLA Ops:
  6.5 2.2 %copy.44 = bf16[128,2560]{0,1:T(8,128)(2,1)} copy(bf16[128,2560]{1,0:T(8,128)(2,1)} %param.15) | data formatting | bytes 1310720 | tf_op args[1]
  8.8 2.2 %copy.46 = bf16[128,2560]{0,1:T(8,128)(2,1)} copy(bf16[128,2560]{1,0:T(8,128)(2,1)} %param.16) | data formatting | bytes 1310720 | tf_op args[2]
  13.4 8.0 %collective-permute-start.6 = (bf16[128,20,128]{0,2,1:T(8,128)(2,1)}, bf16[128,20,128]{0,2,1:T(8,128)(2,1)S(1)}, u32[]{:S(2)}, u32[]{:S(2)}) collective-permute-start(bf16[128,20,128]{0,2,1:T(8,128)(2,1)} %bitcast.29), channel_id=1, source_target_pairs={{0,8},{2,10},{4,12},{6,14},{1,9},{3,11},{5,13},{7,15},{16,24},{18,... | collective-permute-start | bytes 1966088 | tf_op jit(solution)/shard_map/ppermute | solution.py:17
  21.4 1.3 collective-permute-start.4
  22.7 2.6 %collective-permute-start.2 = (bf16[128,20,128]{0,2,1:T(8,128)(2,1)}, bf16[128,20,128]{0,2,1:T(8,128)(2,1)S(1)}, u32[]{:S(2)}, u32[]{:S(2)}) collective-permute-start(bf16[128,20,128]{0,2,1:T(8,128)(2,1)} %bitcast.29), channel_id=1, source_target_pairs={{0,2},{2,4},{4,6},{6,8},{8,10},{10,12},{12,14},{1,3},{3,5},{5,7},{... | collective-permute-start | bytes 1966088 | tf_op jit(solution)/shard_map/ppermute | solution.py:17
  33.1 5.8 %conditional.6 = (f32[128,20,128]{2,0,1:T(8,128)S(1)}, f32[128,20]{0,1:T(8,128)}, f32[128,20]{0,1:T(8,128)S(1)}) conditional(s32[]{:T(128)} %convert_element_type.44, () %tuple.63, (bf16[256,2560]{0,1:T(8,128)(2,1)}, bf16[128,20,128]{0,2,1:T(8,128)(2,1)S(1)}, bf16[256,2560]{0,1:T(8,128)(2,1)}) %tuple.64), branch_computations={%region_4.5_spmd, %region_5.8_spmd} | conditional | flops 340782080 | bytes 17735732 | solution.py:48
  33.1 2.6 %multiply_reduce_fusion.1 = (f32[20,128]{1,0:T(8,128)}, f32[20,128,256]{2,1,0:T(8,128)S(1)}) fusion(bf16[128,20,128]{0,2,1:T(8,128)(2,1)S(1)} %get-tuple-element.124, bf16[256,20,128]{0,2,1:T(8,128)(2,1)} %bitcast.100), kind=kOutput, calls=%fused_computation.9 | convolution fusion | flops 169080320 | bytes 4597760 | tf_op jit(solution)/shard_map/cond/branch_1_fun/qhd,khd->hqk/dot_general | solution.py:23
  35.7 1.6 convolution_bitcast_fusion.1
  37.3 1.5 fusion.6
  38.9 4.8 %collective-permute-start.8 = (f32[128,20,128]{2,0,1:T(8,128)S(1)}, f32[128,20,128]{2,0,1:T(8,128)}, u32[]{:S(2)}, u32[]{:S(2)}) collective-permute-start(f32[128,20,128]{2,0,1:T(8,128)S(1)} %get-tuple-element.96), channel_id=1, source_target_pairs={{0,2},{2,4},{4,6},{6,8},{8,10},{10,12},{12,14},{1,3},{3,5},{5,7},{... | collective-permute-start | bytes 3932168 | tf_op jit(solution)/shard_map/ppermute | solution.py:17
  45.6 17.1 %collective-permute-done.4 = bf16[128,20,128]{0,2,1:T(8,128)(2,1)} collective-permute-done((bf16[128,20,128]{0,2,1:T(8,128)(2,1)}, bf16[128,20,128]{0,2,1:T(8,128)(2,1)}, u32[]{:S(2)}, u32[]{:S(2)}) %collective-permute-start.4) | collective-permute-done | bytes 655392 | tf_op jit(solution)/shard_map/ppermute | solution.py:17
  63.5 1.3 collective-permute-start.5
  64.8 6.0 %conditional.5 = (f32[1,128,20,128]{3,1,2,0:T(8,128)S(1)}, f32[1,128,20]{1,2,0:T(8,128)}, f32[1,128,20]{1,2,0:T(8,128)S(1)}) conditional(s32[]{:T(128)} %bitcast.28, () %tuple.61, (bf16[256,2560]{0,1:T(8,128)(2,1)}, bf16[128,20,128]{0,2,1:T(8,128)(2,1)}, bf16[256,2560]{0,1:T(8,128)(2,1)}) %tuple.62), branch_computations={%region_0.0_spmd, %region_1.0_spmd} | conditional | flops 340782080 | bytes 17735732 | solution.py:48
  64.9 2.9 %multiply_reduce_fusion = (f32[20,128]{1,0:T(8,128)}, f32[20,128,256]{2,1,0:T(8,128)S(1)}) fusion(bf16[128,20,128]{0,2,1:T(8,128)(2,1)} %get-tuple-element.121, bf16[256,20,128]{0,2,1:T(8,128)(2,1)} %bitcast.103), kind=kOutput, calls=%fused_computation.1 | convolution fusion | flops 169080320 | bytes 4597760 | tf_op jit(solution)/shard_map/cond/branch_1_fun/qhd,khd->hqk/dot_general | solution.py:23
  67.7 1.6 convolution_bitcast_fusion
  69.3 1.5 fusion
  75.1 4.5 %collective-permute-start.1 = (f32[128,20]{0,1:T(8,128)}, f32[128,20]{0,1:T(8,128)S(1)}, u32[]{:S(2)}, u32[]{:S(2)}) collective-permute-start(f32[128,20]{0,1:T(8,128)} %get-tuple-element.91), channel_id=1, source_target_pairs={{0,2},{2,4},{4,6},{6,8},{8,10},{10,12},{12,14},{1,3},{3,5},{5,7},{... | collective-permute-start | bytes 30728 | tf_op jit(solution)/shard_map/ppermute | solution.py:17
  81.6 6.3 %collective-permute-start.10 = (f32[128,20,128]{2,0,1:T(8,128)}, f32[128,20,128]{2,0,1:T(8,128)S(1)}, u32[]{:S(2)}, u32[]{:S(2)}) collective-permute-start(f32[128,20,128]{2,0,1:T(8,128)} %copy-done.8), channel_id=1, source_target_pairs={{0,8},{2,10},{4,12},{6,14},{1,9},{3,11},{5,13},{7,15},{16,24},{18,... | collective-permute-start | bytes 3932168 | tf_op jit(solution)/shard_map/ppermute | solution.py:17
  88.0 1.3 collective-permute-start.11
  93.3 26.0 %collective-permute-done.13 = f32[128,20]{0,1:T(8,128)S(1)} collective-permute-done((f32[128,20]{0,1:T(8,128)S(1)}, f32[128,20]{0,1:T(8,128)S(1)}, u32[]{:S(2)}, u32[]{:S(2)}) %collective-permute-start.13) | collective-permute-done | bytes 10272 | tf_op jit(solution)/shard_map/ppermute | solution.py:17
  119.3 52.9 %collective-permute-start.14 = (f32[128,20]{0,1:T(8,128)S(1)}, f32[128,20]{0,1:T(8,128)S(1)}, u32[]{:S(2)}, u32[]{:S(2)}) collective-permute-start(f32[128,20]{0,1:T(8,128)S(1)} %get-tuple-element.103), channel_id=1, source_target_pairs={{0,8},{2,10},{4,12},{6,14},{1,9},{3,11},{5,13},{7,15},{16,24},{18,... | collective-permute-start | bytes 30728 | tf_op jit(solution)/shard_map/ppermute | solution.py:17
  172.2 1.4 collective-permute-done.14
  174.9 5.2 %collective-permute-done.15 = f32[128,20]{0,1:T(8,128)S(1)} collective-permute-done((f32[128,20]{0,1:T(8,128)S(1)}, f32[128,20]{0,1:T(8,128)S(1)}, u32[]{:S(2)}, u32[]{:S(2)}) %collective-permute-start.15) | collective-permute-done | bytes 10272 | tf_op jit(solution)/shard_map/ppermute | solution.py:17
  184.8 4.6 %multiply_reduce_fusion.5 = f32[128,20,128]{2,0,1:T(8,128)S(1)} fusion(f32[5,128,20,128]{3,1,2,0:T(8,128)} %bitcast_dynamic-update-slice_fusion, f32[5,128,20]{1,2,0:T(8,128)S(1)} %get-tuple-element.136), kind=kLoop, calls=%fused_computation.40 | loop fusion | flops 2949120 | bytes 7915520 | tf_op jit(solution)/shard_map/reduce_sum | solution.py:72
  (76 shorter events, 27.5 us)
Async XLA Ops:
  6.5 4.5 %copy-start.9 = (bf16[128,2560]{1,0:T(8,128)(2,1)S(1)}, bf16[128,2560]{1,0:T(8,128)(2,1)}, u32[]{:S(2)}) copy-start(bf16[128,2560]{1,0:T(8,128)(2,1)} %param.14) | copy-start | bytes 1966084
  6.5 18.8 %copy-start.10 = (s32[8,5]{1,0:T(8,128)S(1)}, s32[8,5]{1,0:T(8,128)}, u32[]{:S(2)}) copy-start(s32[8,5]{1,0:T(8,128)} %param.17) | copy-start | bytes 484
  6.5 25.4 %all-gather.3.cloned.1.call-start = ((), (), s32[]{:S(2)}) async-start(), calls=%async_computation | async-start | bytes 1966080 | tf_op jit(solution)/shard_map/all_gather | solution.py:84
  8.8 24.3 %all-gather.5.cloned.1.call-start = ((), (), s32[]{:S(2)}) async-start(), calls=%async_computation.1 | async-start | bytes 1966080 | tf_op jit(solution)/shard_map/all_gather | solution.py:85
  12.1 19.8 %collective-permute-start = (bf16[128,20,128]{0,2,1:T(8,128)(2,1)}, bf16[128,20,128]{0,2,1:T(8,128)(2,1)S(1)}, u32[]{:S(2)}, u32[]{:S(2)}) collective-permute-start(bf16[128,20,128]{0,2,1:T(8,128)(2,1)} %bitcast.29), channel_id=1, source_target_pairs={{2,0},{4,2},{6,4},{8,6},{10,8},{12,10},{14,12},{3,1},{5,3},{7,5},{... | collective-permute-start | bytes 1966088 | tf_op jit(solution)/shard_map/ppermute | solution.py:17
  13.4 30.2 %collective-permute-start.6 = (bf16[128,20,128]{0,2,1:T(8,128)(2,1)}, bf16[128,20,128]{0,2,1:T(8,128)(2,1)S(1)}, u32[]{:S(2)}, u32[]{:S(2)}) collective-permute-start(bf16[128,20,128]{0,2,1:T(8,128)(2,1)} %bitcast.29), channel_id=1, source_target_pairs={{0,8},{2,10},{4,12},{6,14},{1,9},{3,11},{5,13},{7,15},{16,24},{18,... | collective-permute-start | bytes 1966088 | tf_op jit(solution)/shard_map/ppermute | solution.py:17
  21.4 41.3 %collective-permute-start.4 = (bf16[128,20,128]{0,2,1:T(8,128)(2,1)}, bf16[128,20,128]{0,2,1:T(8,128)(2,1)}, u32[]{:S(2)}, u32[]{:S(2)}) collective-permute-start(bf16[128,20,128]{0,2,1:T(8,128)(2,1)} %bitcast.29), channel_id=1, source_target_pairs={{8,0},{10,2},{12,4},{14,6},{9,1},{11,3},{13,5},{15,7},{24,16},{26,... | collective-permute-start | bytes 1966088 | tf_op jit(solution)/shard_map/ppermute | solution.py:17
  22.7 49.3 %collective-permute-start.2 = (bf16[128,20,128]{0,2,1:T(8,128)(2,1)}, bf16[128,20,128]{0,2,1:T(8,128)(2,1)S(1)}, u32[]{:S(2)}, u32[]{:S(2)}) collective-permute-start(bf16[128,20,128]{0,2,1:T(8,128)(2,1)} %bitcast.29), channel_id=1, source_target_pairs={{0,2},{2,4},{4,6},{6,8},{8,10},{10,12},{12,14},{1,3},{3,5},{5,7},{... | collective-permute-start | bytes 1966088 | tf_op jit(solution)/shard_map/ppermute | solution.py:17
  33.1 2.7 %copy-start.2 = (bf16[256,2560]{0,1:T(8,128)(2,1)S(1)}, bf16[256,2560]{0,1:T(8,128)(2,1)}, u32[]{:S(2)}) copy-start(bf16[256,2560]{0,1:T(8,128)(2,1)} %get-tuple-element.65) | copy-start | bytes 3932164 | tf_op jit(solution)/shard_map/cond
  38.9 141.2 %collective-permute-start.8 = (f32[128,20,128]{2,0,1:T(8,128)S(1)}, f32[128,20,128]{2,0,1:T(8,128)}, u32[]{:S(2)}, u32[]{:S(2)}) collective-permute-start(f32[128,20,128]{2,0,1:T(8,128)S(1)} %get-tuple-element.96), channel_id=1, source_target_pairs={{0,2},{2,4},{4,6},{6,8},{8,10},{10,12},{12,14},{1,3},{3,5},{5,7},{... | collective-permute-start | bytes 3932168 | tf_op jit(solution)/shard_map/ppermute | solution.py:17
  44.3 18.4 %copy-start.6 = (f32[128,20,128]{2,0,1:T(8,128)}, f32[128,20,128]{2,0,1:T(8,128)S(1)}, u32[]{:S(2)}) copy-start(f32[128,20,128]{2,0,1:T(8,128)S(1)} %get-tuple-element.99) | copy-start | bytes 3932164
  44.4 36.0 %collective-permute-start.7 = (f32[128,20]{0,1:T(8,128)}, f32[128,20]{0,1:T(8,128)S(1)}, u32[]{:S(2)}, u32[]{:S(2)}) collective-permute-start(f32[128,20]{0,1:T(8,128)} %get-tuple-element.94), channel_id=1, source_target_pairs={{8,0},{10,2},{12,4},{14,6},{9,1},{11,3},{13,5},{15,7},{24,16},{26,... | collective-permute-start | bytes 30728 | tf_op jit(solution)/shard_map/ppermute | solution.py:17
  63.5 18.2 %collective-permute-start.5 = (f32[128,20]{0,1:T(8,128)}, f32[128,20]{0,1:T(8,128)S(1)}, u32[]{:S(2)}, u32[]{:S(2)}) collective-permute-start(f32[128,20]{0,1:T(8,128)} %get-tuple-element.93), channel_id=1, source_target_pairs={{0,8},{2,10},{4,12},{6,14},{1,9},{3,11},{5,13},{7,15},{16,24},{18,... | collective-permute-start | bytes 30728 | tf_op jit(solution)/shard_map/ppermute | solution.py:17
  64.9 2.9 %copy-start.5 = (bf16[256,2560]{0,1:T(8,128)(2,1)S(1)}, bf16[256,2560]{0,1:T(8,128)(2,1)}, u32[]{:S(2)}) copy-start(bf16[256,2560]{0,1:T(8,128)(2,1)} %get-tuple-element.62) | copy-start | bytes 3932164 | tf_op jit(solution)/shard_map/cond
  73.1 14.9 %copy-start.7 = (f32[128,20,128]{2,0,1:T(8,128)S(1)}, f32[128,20,128]{2,0,1:T(8,128)}, u32[]{:S(2)}) copy-start(f32[128,20,128]{2,0,1:T(8,128)} %copy-done.6) | copy-start | bytes 3932164
  73.8 14.2 %collective-permute-start.3 = (f32[128,20]{0,1:T(8,128)}, f32[128,20]{0,1:T(8,128)S(1)}, u32[]{:S(2)}, u32[]{:S(2)}) collective-permute-start(f32[128,20]{0,1:T(8,128)} %get-tuple-element.92), channel_id=1, source_target_pairs={{2,0},{4,2},{6,4},{8,6},{10,8},{12,10},{14,12},{3,1},{5,3},{7,5},{... | collective-permute-start | bytes 30728 | tf_op jit(solution)/shard_map/ppermute | solution.py:17
  75.1 14.2 %collective-permute-start.1 = (f32[128,20]{0,1:T(8,128)}, f32[128,20]{0,1:T(8,128)S(1)}, u32[]{:S(2)}, u32[]{:S(2)}) collective-permute-start(f32[128,20]{0,1:T(8,128)} %get-tuple-element.91), channel_id=1, source_target_pairs={{0,2},{2,4},{4,6},{6,8},{8,10},{10,12},{12,14},{1,3},{3,5},{5,7},{... | collective-permute-start | bytes 30728 | tf_op jit(solution)/shard_map/ppermute | solution.py:17
  80.3 100.9 %collective-permute-start.9 = (f32[128,20,128]{2,0,1:T(8,128)S(1)}, f32[128,20,128]{2,0,1:T(8,128)S(1)}, u32[]{:S(2)}, u32[]{:S(2)}) collective-permute-start(f32[128,20,128]{2,0,1:T(8,128)S(1)} %get-tuple-element.97), channel_id=1, source_target_pairs={{2,0},{4,2},{6,4},{8,6},{10,8},{12,10},{14,12},{3,1},{5,3},{7,5},{... | collective-permute-start | bytes 3932168 | tf_op jit(solution)/shard_map/ppermute | solution.py:17
  81.6 100.8 %collective-permute-start.10 = (f32[128,20,128]{2,0,1:T(8,128)}, f32[128,20,128]{2,0,1:T(8,128)S(1)}, u32[]{:S(2)}, u32[]{:S(2)}) collective-permute-start(f32[128,20,128]{2,0,1:T(8,128)} %copy-done.8), channel_id=1, source_target_pairs={{0,8},{2,10},{4,12},{6,14},{1,9},{3,11},{5,13},{7,15},{16,24},{18,... | collective-permute-start | bytes 3932168 | tf_op jit(solution)/shard_map/ppermute | solution.py:17
  88.0 95.6 %collective-permute-start.11 = (f32[128,20,128]{2,0,1:T(8,128)S(1)}, f32[128,20,128]{2,0,1:T(8,128)S(1)}, u32[]{:S(2)}, u32[]{:S(2)}) collective-permute-start(f32[128,20,128]{2,0,1:T(8,128)S(1)} %copy-done.7), channel_id=1, source_target_pairs={{8,0},{10,2},{12,4},{14,6},{9,1},{11,3},{13,5},{15,7},{24,16},{26,... | collective-permute-start | bytes 3932168 | tf_op jit(solution)/shard_map/ppermute | solution.py:17
  89.3 2.7 %collective-permute-start.12 = (f32[128,20]{0,1:T(8,128)S(1)}, f32[128,20]{0,1:T(8,128)S(1)}, u32[]{:S(2)}, u32[]{:S(2)}) collective-permute-start(f32[128,20]{0,1:T(8,128)S(1)} %get-tuple-element.101), channel_id=1, source_target_pairs={{0,2},{2,4},{4,6},{6,8},{8,10},{10,12},{12,14},{1,3},{3,5},{5,7},{... | collective-permute-start | bytes 30728 | tf_op jit(solution)/shard_map/ppermute | solution.py:17
  92.0 27.4 %collective-permute-start.13 = (f32[128,20]{0,1:T(8,128)S(1)}, f32[128,20]{0,1:T(8,128)S(1)}, u32[]{:S(2)}, u32[]{:S(2)}) collective-permute-start(f32[128,20]{0,1:T(8,128)S(1)} %get-tuple-element.102), channel_id=1, source_target_pairs={{2,0},{4,2},{6,4},{8,6},{10,8},{12,10},{14,12},{3,1},{5,3},{7,5},{... | collective-permute-start | bytes 30728 | tf_op jit(solution)/shard_map/ppermute | solution.py:17
  119.3 54.2 %collective-permute-start.14 = (f32[128,20]{0,1:T(8,128)S(1)}, f32[128,20]{0,1:T(8,128)S(1)}, u32[]{:S(2)}, u32[]{:S(2)}) collective-permute-start(f32[128,20]{0,1:T(8,128)S(1)} %get-tuple-element.103), channel_id=1, source_target_pairs={{0,8},{2,10},{4,12},{6,14},{1,9},{3,11},{5,13},{7,15},{16,24},{18,... | collective-permute-start | bytes 30728 | tf_op jit(solution)/shard_map/ppermute | solution.py:17
  173.6 6.5 %collective-permute-start.15 = (f32[128,20]{0,1:T(8,128)S(1)}, f32[128,20]{0,1:T(8,128)S(1)}, u32[]{:S(2)}, u32[]{:S(2)}) collective-permute-start(f32[128,20]{0,1:T(8,128)S(1)} %get-tuple-element.104), channel_id=1, source_target_pairs={{8,0},{10,2},{12,4},{14,6},{9,1},{11,3},{13,5},{15,7},{24,16},{26,... | collective-permute-start | bytes 30728 | tf_op jit(solution)/shard_map/ppermute | solution.py:17
  (3 other events, 5.3 us)
Sparse Core Ops, SparseCore 0:
  8.9 12.0 all-gather.2
  22.5 10.5 all-gather.4
where the time goes:
time: 197 us; the launch traced here: 198 us
  starting transfers between devices  91.9 us (47%)
  waiting for transfers between devices  51.8 us (26%)
  between operations  19.4 us (10%)
  other arithmetic  13.6 us (7%)
  local copies, waits for them, and re-layouts  12.6 us (6%)
  matrix products  8.67 us (4%)
    ppermute x16, starting transfers between devices, passed_along(): return lax.ppermute(value, axis, pairs)  91.9 us
    ppermute x16, waiting for transfers between devices, passed_along(): return lax.ppermute(value, axis, pairs)  50.6 us
    unnamed x20, local copies, waits for them, and re-layouts  8.36 us
    dot_general x2, matrix products, block_terms(): jnp.einsum('qhd,khd->hqk', query_heads, key_heads, preferred_element_type...  5.5 us
    reduce_sum x1, other arithmetic, combine(): numerator = jnp.sum(factors[..., None] * outs_all, axis=0)  4.58 us
  transfers between devices with their start and end apart: 18, of which 7 were waited for; matrix products, arithmetic and copies ran while one was open for 12% of the time, Pallas kernels for 0%

commit v1 on v0

v1 whole, which is shorter than its diff:
```python
import functools
import math

import jax
import jax.numpy as jnp
from jax import lax
from jax.experimental import pallas as pl
from jax.experimental.pallas import tpu as pltpu
from jax.sharding import PartitionSpec as P

HEADS = 20
HD = 128
TILE_H = 4
OFFSETS = (0, -1, 1, -TILE_H, TILE_H)
GROUP = 1

MESH = pl.DeviceIdType.MESH
FAR = 1e30
TO_EXP2 = math.log2(math.e) / math.sqrt(HD)


def kernel(
    rows, cols, q_hbm, k_hbm, v_hbm, pattern_ref, out_ref,
    q_all, kv, staged, acc, top, total,
    near_send, near_recv, local_sem, far_send, far_recv, out_send, out_recv,
):
    row = lax.axis_index("row")
    col = lax.axis_index("col")
    tokens = q_hbm.shape[0]
    half = q_hbm.shape[1] // cols
    step = GROUP * HD
    chunks = half // step
    own_tokens = pl.ds(pl.multiple_of(col * tokens, tokens), tokens)

    def has(offset):
        if offset == -1:
            return lax.rem(row, TILE_H) != 0
        if offset == 1:
            return (lax.rem(row, TILE_H) != TILE_H - 1) & (row + 1 < rows)
        if offset < 0:
            return row >= -offset
        return row + offset < rows

    def other_col(d):
        return lax.rem(col + d, cols)

    def wide(which, i):
        return pl.ds(pl.multiple_of(which * half + i * step, HD), step)

    def narrow(i):
        return pl.ds(pl.multiple_of(i * step, HD), step)

    barrier = pltpu.get_barrier_semaphore()
    for d in range(1, cols):
        pl.semaphore_signal(barrier, inc=1, device_id={"col": other_col(d)}, device_id_type=MESH)
    for j in range(1, 5):
        @pl.when(has(-OFFSETS[j]))
        def _():
            pl.semaphore_signal(
                barrier, inc=1, device_id={"row": row - OFFSETS[j]}, device_id_type=MESH
            )
    peers = cols - 1
    for j in range(1, 5):
        peers = peers + has(-OFFSETS[j]).astype(jnp.int32)
    pl.semaphore_wait(barrier, peers)

    def near_parts(i):
        return (
            (0, k_hbm, kv.at[0, 0, own_tokens, narrow(i)]),
            (1, v_hbm, kv.at[0, 1, own_tokens, narrow(i)]),
            (2, q_hbm, q_all.at[own_tokens, narrow(i)]),
        )

    def near_copies(i, which):
        for n, src, dst in near_parts(i):
            if n in which:
                for d in range(1, cols):
                    yield pltpu.make_async_remote_copy(
                        src_ref=src.at[:, wide(other_col(d), i)],
                        dst_ref=dst,
                        send_sem=near_send.at[n, d - 1, i],
                        recv_sem=near_recv.at[n, d - 1, i],
                        device_id={"col": other_col(d)},
                        device_id_type=MESH,
                    )

    def local_copies(i, which):
        for n, src, dst in near_parts(i):
            if n in which:
                yield pltpu.make_async_copy(
                    src.at[:, wide(col, i)], dst, local_sem.at[n, i]
                )

    def far_copy(j, i):
        return pltpu.make_async_remote_copy(
            src_ref=kv.at[0, :, :, narrow(i)],
            dst_ref=kv.at[j, :, :, narrow(i)],
            send_sem=far_send.at[j - 1, i],
            recv_sem=far_recv.at[j - 1, i],
            device_id={"row": row - OFFSETS[j]},
            device_id_type=MESH,
        )

    for which in ((0, 1), (2,)):
        @pl.loop(0, chunks)
        def _(i):
            for copy in near_copies(i, which):
                copy.start()
            for copy in local_copies(i, which):
                copy.start()

    @pl.loop(0, chunks)
    def _(i):
        for copy in near_copies(i, (0, 1)):
            copy.wait_recv()
        for copy in local_copies(i, (0, 1)):
            copy.wait()
        for j in (3, 4, 1, 2):
            @pl.when(has(-OFFSETS[j]))
            def _():
                far_copy(j, i).start()

    def out_copies(i):
        for d in range(1, cols):
            to = other_col(d)
            yield pltpu.make_async_remote_copy(
                src_ref=staged.at[pl.ds(pl.multiple_of(to * tokens, tokens), tokens), narrow(i)],
                dst_ref=out_ref.at[:, wide(col, i)],
                send_sem=out_send.at[d - 1, i],
                recv_sem=out_recv.at[d - 1, i],
                device_id={"col": to},
                device_id_type=MESH,
            )

    @pl.loop(0, chunks)
    def _(i):
        for copy in near_copies(i, (2,)):
            copy.wait_recv()
        for copy in local_copies(i, (2,)):
            copy.wait()

        def block(j, g):
            head = pl.ds(pl.multiple_of(i * step + g * HD, HD), HD)
            scores = lax.dot_general(
                q_all[:, head], kv[j, 0, :, head], (((1,), (1,)), ((), ())),
                preferred_element_type=jnp.float32,
            )
            peak = jnp.max(scores, axis=1, keepdims=True)
            if j == 0:
                weights = jnp.exp2((scores - peak) * TO_EXP2)
                here = jnp.sum(weights, axis=1, keepdims=True)
                out = jnp.dot(
                    weights.astype(jnp.bfloat16), kv[j, 1, :, head],
                    preferred_element_type=jnp.float32,
                )
                top[g] = peak
                total[g] = here
                acc[g] = out
            else:
                live = pattern_ref[row, j] == 1
                before = top[g]
                after = jnp.where(live, jnp.maximum(before, peak), before)
                weights = jnp.exp2((scores - jnp.where(live, after, FAR)) * TO_EXP2)
                here = jnp.sum(weights, axis=1, keepdims=True)
                out = jnp.dot(
                    weights.astype(jnp.bfloat16), kv[j, 1, :, head],
                    preferred_element_type=jnp.float32,
                )
                factor = jnp.exp2((before - after) * TO_EXP2)
                top[g] = after
                total[g] = total[g] * factor + here
                acc[g] = acc[g] * factor + out

        for g in range(GROUP):
            block(0, g)
        for j in (1, 2, 3, 4):
            @pl.when(has(OFFSETS[j]))
            def _():
                far_copy(j, i).wait_recv()
                for g in range(GROUP):
                    block(j, g)
        for g in range(GROUP):
            head = pl.ds(pl.multiple_of(i * step + g * HD, HD), HD)
            staged[:, head] = (acc[g] / total[g]).astype(jnp.bfloat16)
        out_ref[:, wide(col, i)] = staged[own_tokens, narrow(i)]
        for copy in out_copies(i):
            copy.start()

    @pl.loop(0, chunks)
    def _(i):
        for copy in near_copies(i, (0, 1, 2)):
            copy.wait_send()
        for j in range(1, 5):
            @pl.when(has(-OFFSETS[j]))
            def _():
                far_copy(j, i).wait_send()
        for copy in out_copies(i):
            copy.wait()


def shards(rows, cols, queries, keys, values, pattern):
    tokens, width = queries.shape
    half = width // cols
    chunks = half // (GROUP * HD)
    whole = tokens * cols
    dma = pltpu.SemaphoreType.DMA
    return pl.pallas_call(
        functools.partial(kernel, rows, cols),
        out_shape=jax.ShapeDtypeStruct((tokens, width), jnp.bfloat16),
        in_specs=[pl.BlockSpec(memory_space=pl.ANY)] * 3
        + [pl.BlockSpec(memory_space=pltpu.SMEM)],
        out_specs=pl.BlockSpec(memory_space=pltpu.VMEM),
        scratch_shapes=[
            pltpu.VMEM((whole, half), jnp.bfloat16),
            pltpu.VMEM((5, 2, whole, half), jnp.bfloat16),
            pltpu.VMEM((whole, half), jnp.bfloat16),
            pltpu.VMEM((GROUP, whole, HD), jnp.float32),
            pltpu.VMEM((GROUP, whole, 1), jnp.float32),
            pltpu.VMEM((GROUP, whole, 1), jnp.float32),
            dma((3, cols - 1, chunks)),
            dma((3, cols - 1, chunks)),
            dma((3, chunks)),
            dma((4, chunks)),
            dma((4, chunks)),
            dma((cols - 1, chunks)),
            dma((cols - 1, chunks)),
        ],
        compiler_params=pltpu.CompilerParams(
            collective_id=0, has_side_effects=True, vmem_limit_bytes=32 * 1024 * 1024
        ),
        cost_estimate=pl.CostEstimate(
            flops=4 * 4 * whole * whole * half,
            bytes_accessed=8 * tokens * width,
            transcendentals=4 * whole * whole * half // HD,
        ),
    )(queries, keys, values, pattern)


def solution(mesh):
    split = P(("groups", "row", "col"), None)
    return jax.shard_map(
        functools.partial(shards, mesh.shape["row"], mesh.shape["col"]),
        mesh=mesh,
        in_specs=(split, split, split, P("groups", None)),
        out_specs=split,
        check_vma=False,
    )
```

time: 197 us -> 73.7 us (0.37)
  starting transfers between devices: 91.9 us -> 0 us
  Pallas kernels: 0 us -> 68.1 us
  waiting for transfers between devices: 51.8 us -> 0 us
  between operations: 19.4 us -> 0.01 us
  other arithmetic: 13.6 us -> 0 us
  matrix products: 8.67 us -> 0 us
  local copies, waits for them, and re-layouts: 12.6 us -> 4.79 us
    ppermute x16 -> x0, starting transfers between devices: 91.9 us -> none  [passed_along(): return lax.ppermute(value, axis, pairs)]
    pallas_call x0 -> x1, Pallas kernels: none -> 68.1 us  [shards(): pl.pallas_call(functools.partial(kernel, rows, cols), out_shape=jax.Shape...]
    ppermute x16 -> x0, waiting for transfers between devices: 50.6 us -> none  [passed_along(): return lax.ppermute(value, axis, pairs)]
    dot_general x4 -> x0, matrix products: 8.67 us -> none  [the longest x2 5.5 us: block_terms(): jnp.einsum('qhd,khd->hqk', query_heads, key_heads, preferred_element_type...]
    reduce_sum x4 -> x0, other arithmetic: 7.7 us -> none  [the longest x1 4.58 us: combine(): numerator = jnp.sum(factors[..., None] * outs_all, axis=0)]
    unnamed x20 -> x9, local copies, waits for them, and re-layouts: 8.36 us -> 4.79 us
    unnamed x8 -> x0, other arithmetic: 3.55 us -> none
    another operation x9 -> x0, local copies, waits for them, and re-layouts: 2.18 us -> none
  transfers between devices with their start and end apart: 18 -> 0, of which waited for: 7 -> 0; matrix products, arithmetic and copies ran while one was open for 12% -> 0% of each run, Pallas kernels for 0% -> 0%
where the time goes in v1:
time: 73.7 us; the launch traced here: 72.9 us
  Pallas kernels  68.1 us (92%)
  local copies, waits for them, and re-layouts  4.79 us (6%)
    pallas_call x1, Pallas kernels, shards(): pl.pallas_call(functools.partial(kernel, rows, cols), out_shape=jax.Shape...  68.1 us
    unnamed x9, local copies, waits for them, and re-layouts  4.79 us

profile of v1, /device:TPU:0, one launch (start us, length us, event | category | flops | bytes accessed | tf_op | source)
XLA Modules:
  0.0 72.9 jit_solution(10388711876564614715)
XLA Ops:
  0.0 0.0 copy-start
  0.0 1.1 %copy-done = bf16[128,2560]{1,0:T(8,128)(2,1)S(1)} copy-done((bf16[128,2560]{1,0:T(8,128)(2,1)S(1)}, bf16[128,2560]{1,0:T(8,128)(2,1)}, u32[]{:S(2)}) %copy-start) | copy-done | bytes 655384
  1.1 0.0 copy-start.1
  1.1 1.1 %copy-done.1 = bf16[128,2560]{1,0:T(8,128)(2,1)S(1)} copy-done((bf16[128,2560]{1,0:T(8,128)(2,1)S(1)}, bf16[128,2560]{1,0:T(8,128)(2,1)}, u32[]{:S(2)}) %copy-start.1) | copy-done | bytes 655384
  2.2 0.0 copy-start.2
  2.2 1.1 %copy-done.2 = bf16[128,2560]{1,0:T(8,128)(2,1)S(1)} copy-done((bf16[128,2560]{1,0:T(8,128)(2,1)S(1)}, bf16[128,2560]{1,0:T(8,128)(2,1)}, u32[]{:S(2)}) %copy-start.2) | copy-done | bytes 655384
  3.3 0.0 copy-start.3
  3.3 0.7 copy-done.3
  4.0 68.1 %shard_map.46 = bf16[128,2560]{1,0:T(8,128)(2,1)S(1)} custom-call(bf16[128,2560]{1,0:T(8,128)(2,1)S(1)} %copy-done, bf16[128,2560]{1,0:T(8,128)(2,1)S(1)} %copy-done.1, bf16[128,2560]{1,0:T(8,128)(2,1)S(1)} %copy-done.2, s32[8,5]{1,0:T(8,128)S(1)} %copy-done.3), custom_call_target="tpu_custom_call" | custom-call | flops 1342177280 | bytes 2621440 | tf_op jit(solution)/shard_map/pallas_call | solution.py:207
  72.1 0.8 %copy.6 = bf16[128,2560]{1,0:T(8,128)(2,1)} copy(bf16[128,2560]{1,0:T(8,128)(2,1)S(1)} %shard_map.46) | data formatting | bytes 1310720
Async XLA Ops:
  0.0 1.1 %copy-start = (bf16[128,2560]{1,0:T(8,128)(2,1)S(1)}, bf16[128,2560]{1,0:T(8,128)(2,1)}, u32[]{:S(2)}) copy-start(bf16[128,2560]{1,0:T(8,128)(2,1)} %q_hbm.1) | copy-start | bytes 1966084
  1.1 1.1 %copy-start.1 = (bf16[128,2560]{1,0:T(8,128)(2,1)S(1)}, bf16[128,2560]{1,0:T(8,128)(2,1)}, u32[]{:S(2)}) copy-start(bf16[128,2560]{1,0:T(8,128)(2,1)} %k_hbm.1) | copy-start | bytes 1966084
  2.2 1.1 %copy-start.2 = (bf16[128,2560]{1,0:T(8,128)(2,1)S(1)}, bf16[128,2560]{1,0:T(8,128)(2,1)}, u32[]{:S(2)}) copy-start(bf16[128,2560]{1,0:T(8,128)(2,1)} %v_hbm.1) | copy-start | bytes 1966084
  3.3 0.7 copy-start.3

commit v2 on v1

--- a/solution.py
+++ b/solution.py
@@ -12,7 +12,7 @@
 HD = 128
 TILE_H = 4
 OFFSETS = (0, -1, 1, -TILE_H, TILE_H)
-GROUP = 1
+GROUP = 2
 
 MESH = pl.DeviceIdType.MESH
 FAR = 1e30
@@ -56,12 +56,15 @@
     for j in range(1, 5):
         @pl.when(has(-OFFSETS[j]))
         def _():
-            pl.semaphore_signal(
-                barrier, inc=1, device_id={"row": row - OFFSETS[j]}, device_id_type=MESH
-            )
+            for d in range(cols):
+                pl.semaphore_signal(
+                    barrier, inc=1,
+                    device_id={"row": row - OFFSETS[j], "col": other_col(d)},
+                    device_id_type=MESH,
+                )
     peers = cols - 1
     for j in range(1, 5):
-        peers = peers + has(-OFFSETS[j]).astype(jnp.int32)
+        peers = peers + cols * has(-OFFSETS[j]).astype(jnp.int32)
     pl.semaphore_wait(barrier, peers)
 
     def near_parts(i):
@@ -91,34 +94,29 @@
                     src.at[:, wide(col, i)], dst, local_sem.at[n, i]
                 )
 
-    def far_copy(j, i):
-        return pltpu.make_async_remote_copy(
-            src_ref=kv.at[0, :, :, narrow(i)],
-            dst_ref=kv.at[j, :, :, narrow(i)],
-            send_sem=far_send.at[j - 1, i],
-            recv_sem=far_recv.at[j - 1, i],
-            device_id={"row": row - OFFSETS[j]},
-            device_id_type=MESH,
-        )
-
-    for which in ((0, 1), (2,)):
-        @pl.loop(0, chunks)
-        def _(i):
-            for copy in near_copies(i, which):
-                copy.start()
-            for copy in local_copies(i, which):
-                copy.start()
+    def far_copies(j, i):
+        for d in range(cols):
+            for n, src in ((0, k_hbm), (1, v_hbm)):
+                yield pltpu.make_async_remote_copy(
+                    src_ref=src.at[:, wide(other_col(d), i)],
+                    dst_ref=kv.at[j, n, own_tokens, narrow(i)],
+                    send_sem=far_send.at[j - 1, n, d, i],
+                    recv_sem=far_recv.at[j - 1, n, d, i],
+                    device_id={"row": row - OFFSETS[j], "col": other_col(d)},
+                    device_id_type=MESH,
+                )
 
     @pl.loop(0, chunks)
     def _(i):
-        for copy in near_copies(i, (0, 1)):
-            copy.wait_recv()
-        for copy in local_copies(i, (0, 1)):
-            copy.wait()
         for j in (3, 4, 1, 2):
             @pl.when(has(-OFFSETS[j]))
             def _():
-                far_copy(j, i).start()
+                for copy in far_copies(j, i):
+                    copy.start()
+        for copy in near_copies(i, (0, 1, 2)):
+            copy.start()
+        for copy in local_copies(i, (0, 1, 2)):
+            copy.start()
 
     def out_copies(i):
         for d in range(1, cols):
@@ -134,9 +132,9 @@
 
     @pl.loop(0, chunks)
     def _(i):
-        for copy in near_copies(i, (2,)):
+        for copy in near_copies(i, (0, 1, 2)):
             copy.wait_recv()
-        for copy in local_copies(i, (2,)):
+        for copy in local_copies(i, (0, 1, 2)):
             copy.wait()
 
         def block(j, g):
@@ -176,7 +174,8 @@
         for j in (1, 2, 3, 4):
             @pl.when(has(OFFSETS[j]))
             def _():
-                far_copy(j, i).wait_recv()
+                for copy in far_copies(j, i):
+                    copy.wait_recv()
                 for g in range(GROUP):
                     block(j, g)
         for g in range(GROUP):
@@ -193,7 +192,8 @@
         for j in range(1, 5):
             @pl.when(has(-OFFSETS[j]))
             def _():
-                far_copy(j, i).wait_send()
+                for copy in far_copies(j, i):
+                    copy.wait_send()
         for copy in out_copies(i):
             copy.wait()
 
@@ -207,7 +207,7 @@
     return pl.pallas_call(
         functools.partial(kernel, rows, cols),
         out_shape=jax.ShapeDtypeStruct((tokens, width), jnp.bfloat16),
-        in_specs=[pl.BlockSpec(memory_space=pl.ANY)] * 3
+        in_specs=[pl.BlockSpec(memory_space=pltpu.HBM)] * 3
         + [pl.BlockSpec(memory_space=pltpu.SMEM)],
         out_specs=pl.BlockSpec(memory_space=pltpu.VMEM),
         scratch_shapes=[
@@ -220,13 +220,13 @@
             dma((3, cols - 1, chunks)),
             dma((3, cols - 1, chunks)),
             dma((3, chunks)),
-            dma((4, chunks)),
-            dma((4, chunks)),
+            dma((4, 2, cols, chunks)),
+            dma((4, 2, cols, chunks)),
             dma((cols - 1, chunks)),
             dma((cols - 1, chunks)),
         ],
         compiler_params=pltpu.CompilerParams(
-            collective_id=0, has_side_effects=True, vmem_limit_bytes=32 * 1024 * 1024
+            collective_id=0, has_side_effects=True, vmem_limit_bytes=60 * 1024 * 1024
         ),
         cost_estimate=pl.CostEstimate(
             flops=4 * 4 * whole * whole * half,

time: 73.7 us -> 71.3 us (0.967)
  local copies, waits for them, and re-layouts: 4.79 us -> 1.97 us
    unnamed x9 -> x1, local copies, waits for them, and re-layouts: 4.79 us -> 1.97 us
where the time goes in v2:
time: 71.3 us; the launch traced here: 70.2 us
  Pallas kernels  68.3 us (96%)
  local copies, waits for them, and re-layouts  1.97 us (3%)
    pallas_call x1, Pallas kernels, shards(): pl.pallas_call(functools.partial(kernel, rows, cols), out_shape=jax.Shape...  68.3 us
    unnamed x1, local copies, waits for them, and re-layouts  1.97 us

profile of v2, /device:TPU:0, one launch (start us, length us, event | category | flops | bytes accessed | tf_op | source)
XLA Modules:
  0.0 70.2 jit_solution(1148628433609910499)
XLA Ops:
  0.0 68.3 %shard_map.46 = bf16[128,2560]{1,0:T(8,128)(2,1)} custom-call(bf16[128,2560]{1,0:T(8,128)(2,1)} %q_hbm.1, bf16[128,2560]{1,0:T(8,128)(2,1)} %k_hbm.1, bf16[128,2560]{1,0:T(8,128)(2,1)} %v_hbm.1, s32[8,5]{1,0:T(8,128)} %pattern_ref.1), custom_call_target="tpu_custom_call" | custom-call | flops 1342177280 | bytes 2621440 | tf_op jit(solution)/shard_map/pallas_call | solution.py:207
  68.3 2.0 %copy.6 = bf16[128,2560]{1,0:T(8,128)(2,1)} copy(bf16[128,2560]{1,0:T(8,128)(2,1)} %shard_map.46) | data formatting | bytes 1310720

commit v3 on v2

--- a/solution.py
+++ b/solution.py
@@ -20,9 +20,9 @@
 
 
 def kernel(
-    rows, cols, q_hbm, k_hbm, v_hbm, pattern_ref, out_ref,
+    rows, cols, q_hbm, k_hbm, v_hbm, pattern_hbm, out_ref,
     q_all, kv, staged, acc, top, total,
-    near_send, near_recv, local_sem, far_send, far_recv, out_send, out_recv,
+    pattern_ref, pattern_sem, near_send, near_recv, local_sem, far_send, far_recv, out_send, out_recv,
 ):
     row = lax.axis_index("row")
     col = lax.axis_index("col")
@@ -49,6 +49,9 @@
 
     def narrow(i):
         return pl.ds(pl.multiple_of(i * step, HD), step)
+
+    fetch = pltpu.make_async_copy(pattern_hbm, pattern_ref, pattern_sem)
+    fetch.start()
 
     barrier = pltpu.get_barrier_semaphore()
     for d in range(1, cols):
@@ -108,15 +111,28 @@
 
     @pl.loop(0, chunks)
     def _(i):
-        for j in (3, 4, 1, 2):
+        for j in (3, 4):
             @pl.when(has(-OFFSETS[j]))
             def _():
                 for copy in far_copies(j, i):
                     copy.start()
+
+    @pl.loop(0, chunks)
+    def _(i):
         for copy in near_copies(i, (0, 1, 2)):
             copy.start()
         for copy in local_copies(i, (0, 1, 2)):
             copy.start()
+
+    @pl.loop(0, chunks)
+    def _(i):
+        for j in (1, 2):
+            @pl.when(has(-OFFSETS[j]))
+            def _():
+                for copy in far_copies(j, i):
+                    copy.start()
+
+    fetch.wait()
 
     def out_copies(i):
         for d in range(1, cols):
@@ -208,7 +224,7 @@
         functools.partial(kernel, rows, cols),
         out_shape=jax.ShapeDtypeStruct((tokens, width), jnp.bfloat16),
         in_specs=[pl.BlockSpec(memory_space=pltpu.HBM)] * 3
-        + [pl.BlockSpec(memory_space=pltpu.SMEM)],
+        + [pl.BlockSpec(memory_space=pltpu.HBM)],
         out_specs=pl.BlockSpec(memory_space=pltpu.VMEM),
         scratch_shapes=[
             pltpu.VMEM((whole, half), jnp.bfloat16),
@@ -217,6 +233,8 @@
             pltpu.VMEM((GROUP, whole, HD), jnp.float32),
             pltpu.VMEM((GROUP, whole, 1), jnp.float32),
             pltpu.VMEM((GROUP, whole, 1), jnp.float32),
+            pltpu.SMEM(pattern.shape, pattern.dtype),
+            dma(()),
             dma((3, cols - 1, chunks)),
             dma((3, cols - 1, chunks)),
             dma((3, chunks)),

time: 71.3 us -> 70.3 us (0.986)
  Pallas kernels: 68.3 us -> 67.4 us
    pallas_call x1, Pallas kernels: 68.3 us -> 67.4 us  [shards(): pl.pallas_call(functools.partial(kernel, rows, cols), out_shape=jax.Shape...]
where the time goes in v3:
time: 70.3 us; the launch traced here: 69.4 us
  Pallas kernels  67.4 us (96%)
  local copies, waits for them, and re-layouts  1.97 us (3%)
    pallas_call x1, Pallas kernels, shards(): pl.pallas_call(functools.partial(kernel, rows, cols), out_shape=jax.Shape...  67.4 us
    unnamed x1, local copies, waits for them, and re-layouts  1.97 us

profile of v3, /device:TPU:0, one launch (start us, length us, event | category | flops | bytes accessed | tf_op | source)
XLA Modules:
  0.0 69.4 jit_solution(6245355315753914228)
XLA Ops:
  0.0 67.4 %shard_map.46 = bf16[128,2560]{1,0:T(8,128)(2,1)} custom-call(bf16[128,2560]{1,0:T(8,128)(2,1)} %q_hbm.1, bf16[128,2560]{1,0:T(8,128)(2,1)} %k_hbm.1, bf16[128,2560]{1,0:T(8,128)(2,1)} %v_hbm.1, s32[8,5]{1,0:T(8,128)} %pattern_hbm.1), custom_call_target="tpu_custom_call" | custom-call | flops 1342177280 | bytes 2621440 | tf_op jit(solution)/shard_map/pallas_call | solution.py:223
  67.4 2.0 %copy.6 = bf16[128,2560]{1,0:T(8,128)(2,1)} copy(bf16[128,2560]{1,0:T(8,128)(2,1)} %shard_map.46) | data formatting | bytes 1310720

commit v4 on v3

--- a/solution.py
+++ b/solution.py
@@ -22,7 +22,7 @@
 def kernel(
     rows, cols, q_hbm, k_hbm, v_hbm, pattern_hbm, out_ref,
     q_all, kv, staged, acc, top, total,
-    pattern_ref, pattern_sem, near_send, near_recv, local_sem, far_send, far_recv, out_send, out_recv,
+    pattern_ref, pattern_sem, passed_send, near_send, near_recv, local_sem, far_send, far_recv, out_send, out_recv,
 ):
     row = lax.axis_index("row")
     col = lax.axis_index("col")
@@ -52,6 +52,30 @@
 
     fetch = pltpu.make_async_copy(pattern_hbm, pattern_ref, pattern_sem)
     fetch.start()
+
+    passed = chunks // 2 if TILE_H == 4 and rows % TILE_H == 0 else 0
+    place = lax.rem(row, TILE_H)
+
+    def sends(j, i):
+        if j > 2 or passed == 0:
+            return has(-OFFSETS[j])
+        return has(-OFFSETS[j]) & ((place != j) | (i >= passed))
+
+    def passes(j):
+        return place == (TILE_H - 1 if j == 1 else 0)
+
+    def pass_copies(j, i):
+        for d in range(cols):
+            for n in range(2):
+                part = (n, pl.ds(d * tokens, tokens), narrow(i))
+                yield pltpu.make_async_remote_copy(
+                    src_ref=kv.at[(j,) + part],
+                    dst_ref=kv.at[(3 - j,) + part],
+                    send_sem=passed_send.at[n, d, i],
+                    recv_sem=far_recv.at[2 - j, n, d, i],
+                    device_id={"row": row + 2 * OFFSETS[j]},
+                    device_id_type=MESH,
+                )
 
     barrier = pltpu.get_barrier_semaphore()
     for d in range(1, cols):
@@ -66,6 +90,14 @@
                     device_id_type=MESH,
                 )
     peers = cols - 1
+    if passed:
+        for at, to in ((1, 2), (2, -2)):
+            @pl.when(place == at)
+            def _():
+                pl.semaphore_signal(
+                    barrier, inc=1, device_id={"row": row + to}, device_id_type=MESH
+                )
+        peers = peers + passes(1).astype(jnp.int32) + passes(2).astype(jnp.int32)
     for j in range(1, 5):
         peers = peers + cols * has(-OFFSETS[j]).astype(jnp.int32)
     pl.semaphore_wait(barrier, peers)
@@ -127,7 +159,7 @@
     @pl.loop(0, chunks)
     def _(i):
         for j in (1, 2):
-            @pl.when(has(-OFFSETS[j]))
+            @pl.when(sends(j, i))
             def _():
                 for copy in far_copies(j, i):
                     copy.start()
@@ -192,6 +224,11 @@
             def _():
                 for copy in far_copies(j, i):
                     copy.wait_recv()
+                if j in (1, 2):
+                    @pl.when(passes(j) & (i < passed))
+                    def _():
+                        for copy in pass_copies(j, i):
+                            copy.start()
                 for g in range(GROUP):
                     block(j, g)
         for g in range(GROUP):
@@ -206,9 +243,14 @@
         for copy in near_copies(i, (0, 1, 2)):
             copy.wait_send()
         for j in range(1, 5):
-            @pl.when(has(-OFFSETS[j]))
+            @pl.when(sends(j, i))
             def _():
                 for copy in far_copies(j, i):
+                    copy.wait_send()
+        for j in (1, 2):
+            @pl.when(passes(j) & (i < passed))
+            def _():
+                for copy in pass_copies(j, i):
                     copy.wait_send()
         for copy in out_copies(i):
             copy.wait()
@@ -235,6 +277,7 @@
             pltpu.VMEM((GROUP, whole, 1), jnp.float32),
             pltpu.SMEM(pattern.shape, pattern.dtype),
             dma(()),
+            dma((2, cols, chunks)),
             dma((3, cols - 1, chunks)),
             dma((3, cols - 1, chunks)),
             dma((3, chunks)),

time: 70.3 us -> 69.6 us (0.990); the launches traced: 69.4 us -> 69.5 us
  no operation moved by 1% of the time
where the time goes in v4:
time: 69.6 us; the launch traced here: 69.5 us
  Pallas kernels  67.5 us (97%)
  local copies, waits for them, and re-layouts  1.97 us (3%)
    pallas_call x1, Pallas kernels, shards(): pl.pallas_call(functools.partial(kernel, rows, cols), out_shape=jax.Shape...  67.5 us
    unnamed x1, local copies, waits for them, and re-layouts  1.97 us

profile of v4, /device:TPU:0, one launch (start us, length us, event | category | flops | bytes accessed | tf_op | source)
XLA Modules:
  0.0 69.5 jit_solution(3202280991751074538)
XLA Ops:
  0.0 67.5 %shard_map.46 = bf16[128,2560]{1,0:T(8,128)(2,1)} custom-call(bf16[128,2560]{1,0:T(8,128)(2,1)} %q_hbm.1, bf16[128,2560]{1,0:T(8,128)(2,1)} %k_hbm.1, bf16[128,2560]{1,0:T(8,128)(2,1)} %v_hbm.1, s32[8,5]{1,0:T(8,128)} %pattern_hbm.1), custom_call_target="tpu_custom_call" | custom-call | flops 1342177280 | bytes 2621440 | tf_op jit(solution)/shard_map/pallas_call | solution.py:265
  67.5 2.0 %copy.6 = bf16[128,2560]{1,0:T(8,128)(2,1)} copy(bf16[128,2560]{1,0:T(8,128)(2,1)} %shard_map.46) | data formatting | bytes 1310720
